TPU v7x, 256 devices: a whole 4x4x8 slice. The times are simulated.
256 devices in a mesh: dp: 16 (over z, core), fsdp: 16 (over y, x).
Axes of the slice: x: 4, y: 4, z: 8, core: 2. Of those that a mesh axis runs over, the one named last changes fastest.
Arguments:
- grads: bfloat16 [16, 128, 2560, 128], P('dp', None, 'fsdp'), may hold values from -1400 to 1400
- owner: int32 [128, 1], replicated, may hold values from 0 to 15; in each aligned block of 8 rows (0 to 7, 8 to 15, ...) at most 2 rows name the same one
- momentum: float32 [16, 16, 2, 2560, 128], P('dp', 'fsdp'), may hold values from -24 to 24
Outputs:
- update: float32 [128, 2560, 128], P('dp', 'fsdp')
- new_momentum: float32 [16, 16, 2, 2560, 128], P('dp', 'fsdp')
Inputs may be any that keep to these rules, and one draw needn't show every extreme that they name: Among the 8 blocks of one index of dp at most 2 have the same owner; in some index of dp one owner has exactly 2.
All inputs are finite; a program needn't handle non-finite values.
Results may differ from a plain program's by a relative error of at most 0.0003.
Values may be sent and summed in bfloat16 or wider, within the bound.
A program may use at most 64 MiB of HBM per device.

v0:
```python
import math

import jax
import jax.numpy as jnp
from jax import lax
from jax.sharding import PartitionSpec as P

D = 2560
ITERS = 3


COEF_A = 3.4445
COEF_B = -4.775
COEF_C = 2.0315
MOMENTUM_RATE = 0.95


def poly_step(iterate, gram_now):
    poly_term = COEF_B * gram_now + COEF_C * jnp.einsum(
        "mrs,mst->mrt", gram_now, gram_now, precision=lax.Precision.HIGHEST
    )
    return COEF_A * iterate + jnp.einsum(
        "mdr,mrs->mds", iterate, poly_term, precision=lax.Precision.HIGHEST
    )


def local_gram(iterate):
    return jnp.einsum("mdr,mds->mrs", iterate, iterate, precision=lax.Precision.HIGHEST)


def local(grads, owner, momentum):
    n_dp = lax.axis_size("dp")
    n_fsdp = lax.axis_size("fsdp")
    slots_per = momentum.shape[2]
    block_count = grads.shape[1] // n_dp
    feat_rows = grads.shape[2]
    head_rows = grads.shape[3]
    summed = lax.psum_scatter(grads[0].astype(jnp.float32), "dp", scatter_dimension=0, tiled=True)
    gradient = summed / n_dp
    group_index = lax.axis_index("dp")
    owner_local = lax.dynamic_slice_in_dim(owner[:, 0], group_index * block_count, block_count)
    columns = jnp.arange(block_count, dtype=jnp.int32)
    earlier = (owner_local[:, None] == owner_local[None, :]) & (columns[None, :] < columns[:, None])
    position = jnp.sum(earlier.astype(jnp.int32), axis=1)
    slot_id = owner_local * slots_per + position
    dispatch = (
        slot_id[None, :] == jnp.arange(n_fsdp * slots_per, dtype=jnp.int32)[:, None]
    ).astype(jnp.float32)
    outgoing = jnp.einsum("sm,mdr->sdr", dispatch, gradient, precision=lax.Precision.HIGHEST)
    outgoing = outgoing.reshape(n_fsdp, slots_per, feat_rows, head_rows)
    gathered = lax.all_to_all(outgoing, "fsdp", split_axis=0, concat_axis=2, tiled=True)[0]
    previous = momentum[0, 0]
    renewed = MOMENTUM_RATE * previous + gathered
    velocity = gathered + MOMENTUM_RATE * renewed
    frob_norm = jnp.sqrt(jnp.sum(velocity * velocity, axis=(1, 2), keepdims=True))
    iterate = velocity / (frob_norm + 1e-07)
    for sweep in range(ITERS):
        iterate = poly_step(iterate, local_gram(iterate))
    full_update = 0.2 * math.sqrt(D) * iterate
    returned = lax.all_to_all(full_update[None], "fsdp", split_axis=2, concat_axis=0, tiled=True)
    returned = returned.reshape(n_fsdp * slots_per, feat_rows, head_rows)
    update = jnp.einsum("sm,sdr->mdr", dispatch, returned, precision=lax.Precision.HIGHEST)
    return (update, renewed[None, None])


def solution(mesh):
    return jax.shard_map(
        local,
        mesh=mesh,
        in_specs=(P("dp", None, "fsdp", None), P(), P("dp", "fsdp", None, None, None)),
        out_specs=(P("dp", "fsdp", None), P("dp", "fsdp", None, None, None)),
        check_vma=False,
    )
```

profile of v0, /device:TPU:97, one launch (start us, length us, event | category | flops | bytes accessed | tf_op | source)
XLA Modules:
  0.0 220.2 jit_solution(3896603463252708669)
XLA Ops:
  7.2 7.9 %bitcast_convert_fusion = f32[128,160,128]{2,1,0:T(8,128)} fusion(bf16[1,128,160,128]{3,2,1,0:T(8,128)(2,1)} %param.3), kind=kLoop, calls=%fused_computation | loop fusion | flops 2621440 | bytes 15728640 | tf_op jit(solution)/shard_map/convert_element_type | solution.py:38
  15.2 0.6 copy-done.1
  16.1 75.4 %reduce-scatter.2.cloned.1.call-done = f32[8,160,128]{2,1,0:T(8,128)} async-done(((f32[128,160,128]{2,1,0:T(8,128)}), f32[8,160,128]{2,1,0:T(8,128)}) %reduce-scatter.2.cloned.1.call-update) | async-done | bytes 655376 | tf_op jit(solution)/shard_map/reduce_scatter | solution.py:38
  91.5 1.1 broadcast_multiply_fusion.1
  92.7 1.4 fusion.10
  94.1 1.3 copy.37
  95.4 39.0 %all_to_all.30 = f32[16,2,160,128]{3,1,2,0:T(2,128)S(1)} all-to-all(f32[16,2,160,128]{3,1,2,0:T(2,128)S(1)} %copy.37), channel_id=1, replica_groups=mesh['dp'=16,'fsdp'=16] {'fsdp'}, dimensions={0} | all-to-all | bytes 5242880 | tf_op jit(solution)/shard_map/all_to_all | solution.py:51
  134.4 0.3 copy.38
  134.7 1.4 copy-done
  136.1 1.8 fusion.19
  138.0 0.7 fusion.5
  138.6 0.5 fusion.3
  139.1 4.4 %fusion.20 = f32[2,128,128]{2,1,0:T(8,128)S(1)} fusion(f32[2,2560,128]{2,1,0:T(8,128)S(1)} %fusion.3), kind=kOutput, calls=%fused_computation.37 | convolution fusion | flops 1006632960 | bytes 2752512 | tf_op jit(solution)/shard_map/mdr,mds->mrs/dot_general | solution.py:28
  143.5 0.3 fusion.9
  143.8 2.7 %convolution_add_fusion.2 = f32[2,2560,128]{2,1,0:T(8,128)S(1)} fusion(f32[2,2560,128]{2,1,0:T(8,128)S(1)} %fusion.3, f32[2,128,128]{2,1,0:T(8,128)S(1)} %fusion.9), kind=kOutput, calls=%fused_computation.4 | convolution fusion | flops 1007943680 | bytes 5373952 | tf_op jit(solution)/shard_map/mdr,mrs->mds/dot_general | solution.py:22
  146.5 4.6 %fusion.21 = f32[2,128,128]{2,1,0:T(8,128)S(1)} fusion(f32[2,2560,128]{2,1,0:T(8,128)S(1)} %convolution_add_fusion.2), kind=kOutput, calls=%fused_computation.38 | convolution fusion | flops 1006632960 | bytes 2752512 | tf_op jit(solution)/shard_map/mdr,mds->mrs/dot_general | solution.py:28
  151.4 2.7 %convolution_add_fusion.1 = f32[2,2560,128]{2,1,0:T(8,128)S(1)} fusion(f32[2,2560,128]{2,1,0:T(8,128)S(1)} %convolution_add_fusion.2, f32[2,128,128]{2,1,0:T(8,128)S(1)} %fusion.8), kind=kOutput, calls=%fused_computation.3 | convolution fusion | flops 1007943680 | bytes 5373952 | tf_op jit(solution)/shard_map/mdr,mrs->mds/dot_general | solution.py:22
  154.1 4.4 %fusion.22 = f32[2,128,128]{2,1,0:T(8,128)S(1)} fusion(f32[2,2560,128]{2,1,0:T(8,128)S(1)} %convolution_add_fusion.1), kind=kOutput, calls=%fused_computation.39 | convolution fusion | flops 1006632960 | bytes 2752512 | tf_op jit(solution)/shard_map/mdr,mds->mrs/dot_general | solution.py:28
  158.8 2.9 %fusion.1 = f32[1,2,2560,128]{3,2,1,0:T(8,128)S(1)} fusion(f32[2,2560,128]{2,1,0:T(8,128)S(1)} %convolution_add_fusion.1, f32[2,128,128]{2,1,0:T(8,128)S(1)} %fusion.7), kind=kOutput, calls=%fused_computation.5 | convolution fusion | flops 1008599040 | bytes 5373952 | tf_op jit(solution)/shard_map/mdr,mrs->mds/dot_general | solution.py:22
  161.7 9.8 %copy.42 = f32[1,2,2560,128]{3,1,0,2:T(2,128)S(1)} copy(f32[1,2,2560,128]{3,2,1,0:T(8,128)S(1)} %fusion.1) | data formatting | bytes 5242880 | tf_op jit(solution)/shard_map/broadcast_in_dim | solution.py:60
  171.5 38.4 %all_to_all.31 = f32[1,2,2560,128]{3,1,0,2:T(2,128)S(1)} all-to-all(f32[1,2,2560,128]{3,1,0,2:T(2,128)S(1)} %copy.42), channel_id=1, replica_groups=mesh['dp'=16,'fsdp'=16] {'fsdp'}, dimensions={2} | all-to-all | bytes 5242880 | tf_op jit(solution)/shard_map/all_to_all | solution.py:60
  209.9 1.5 copy.43
  211.4 1.0 fusion.14
  212.4 1.0 copy.44
  (10 shorter events, 0.9 us)
Async XLA Ops:
  7.2 84.4 %reduce-scatter.2.cloned.1.call-start = ((), (), s32[]{:S(2)}) async-start(), calls=%async_computation.3 | async-start | bytes 11141120 | tf_op jit(solution)/shard_map/reduce_scatter | solution.py:38
  15.1 0.7 copy-start.1
  134.4 1.7 copy-start
Sparse Core Ops, SparseCore 0:
  15.3 76.2 reduce-scatter.1
where the time goes:
time: 220 us
  blocking collectives  77.3 us (35%)
  waiting for transfers between devices  75.4 us (34%)
  matrix products  24.9 us (11%)
  local copies, waits for them, and re-layouts  16 us (7%)
  between operations  14.2 us (6%)
  other arithmetic  12.3 us (6%)
    reduce_scatter x1, waiting for transfers between devices, local(): lax.psum_scatter(grads[0].astype(jnp.float32), 'dp', scatter_dimension=0,...  75.4 us
    all_to_all x1, blocking collectives, local(): lax.all_to_all(outgoing, 'fsdp', split_axis=0, concat_axis=2, tiled=True)[0]  39 us
    all_to_all x1, blocking collectives, local(): lax.all_to_all(full_update[None], 'fsdp', split_axis=2, concat_axis=0, ti...  38.4 us
    dot_general x3, matrix products, local_gram(): jnp.einsum('mdr,mds->mrs', iterate, iterate, precision=lax.Precision.HIGH...  13.4 us
    broadcast_in_dim x1, local copies, waits for them, and re-layouts, local(): full_update[None]  9.82 us
    dot_general x3, matrix products, poly_step(): jnp.einsum('mdr,mrs->mds', iterate, poly_term, precision=lax.Precision.HI...  8.33 us
    convert_element_type x1, other arithmetic, local(): grads[0].astype(jnp.float32)  7.93 us
  transfers between devices with their start and end apart: 1, of which 1 were waited for; matrix products, arithmetic and copies ran while one was open for 0% of the time, Pallas kernels for 0%

commit v1 on v0

v1 whole, which is shorter than its diff:
```python
import math

import jax
import jax.numpy as jnp
from jax import lax
from jax.experimental import pallas as pl
from jax.experimental.pallas import tpu as pltpu
from jax.sharding import PartitionSpec as P

MESH = pl.DeviceIdType.MESH
F32 = jnp.float32

NZ = 8
NY = 4
NX = 4
NF = NY * NX
BLOCKS = 8
SLOTS = 2
D = 2560
R = 128
PIECE = D // NF
CHUNK = 32
HALF = CHUNK // 2
NCH = PIECE // CHUNK
EARLY = PIECE - CHUNK
ITERS = 3

COEF_A = 3.4445
COEF_B = -4.775
COEF_C = 2.0315
RATE = 0.95

OFFSETS = ((2, 2), (0, 2), (2, 0), (1, 2), (2, 1), (3, 2), (2, 3), (1, 1), (3, 3), (1, 3), (3, 1), (0, 1), (1, 0), (0, 3), (3, 0))
SIB_ORDER = (4, 3, 5, 2, 6, 1, 7, 0)
RIGHT, LEFT = 0, 1


def dot(a, b):
    return lax.dot_general(a, b, (((1,), (0,)), ((), ())), precision=lax.Precision.HIGHEST, preferred_element_type=F32)


def dot_t(a, b):
    return lax.dot_general(a, b, (((0,), (0,)), ((), ())), precision=lax.Precision.HIGHEST, preferred_element_type=F32)


def polynomial(gram):
    rows = lax.broadcasted_iota(jnp.int32, (R, R), 0)
    cols = lax.broadcasted_iota(jnp.int32, (R, R), 1)
    eye = jnp.where(rows == cols, 1.0, 0.0).astype(F32)
    total = jnp.sum(jnp.sum(gram * eye, axis=1, keepdims=True), axis=0, keepdims=True)
    inv = 1.0 / (jnp.sqrt(total) + 1e-07)
    gram = (gram * inv) * inv
    product = None
    for sweep in range(ITERS):
        poly = COEF_A * eye + COEF_B * gram + COEF_C * dot(gram, gram)
        product = poly if product is None else dot(product, poly)
        if sweep < ITERS - 1:
            gram = dot(poly, dot(gram, poly))
    return (0.2 * math.sqrt(D)) * inv * product


def kernel(
    grads, owner, mom, update, grad_out,
    own, sib, s0, rz, mrecv, gbuf, vbuf, sendg, gsend, grecv, rrecv, qbuf, idx_tab, val_tab,
    own_sem, sib_ssem, sib_rsem, z_ssem, z_rsem, m_ssem, m_rsem, m_lsem, g_ssem, g_rsem, g_lsem,
    p_ssem, p_rsem, r_ssem, r_rsem, q_ssem, q_rsem,
):
    group = lax.axis_index("dp")
    f = lax.axis_index("fsdp")
    z, c = group // 2, group % 2
    y, x = f // NX, f % NX

    def z_of(step):
        return (z + step) % NZ

    def plane(dy, dx):
        return ((y + dy) % NY) * NX + (x + dx) % NX

    sibling = (z * 2 + 1 - c, f)
    z_dev = ((z_of(1) * 2 + c, f), (z_of(NZ - 1) * 2 + c, f))

    own_copy = [pltpu.make_async_copy(grads.at[z_of(j), c], own.at[z_of(j)], own_sem.at[j]) for j in range(NZ)]
    for j in SIB_ORDER:
        own_copy[j].start()
    mom_local = pltpu.make_async_copy(mom.at[:, pl.ds(f * PIECE, PIECE)], mrecv.at[f], m_lsem)
    mom_local.start()

    barrier = pltpu.get_barrier_semaphore()
    for peer in (sibling,) + z_dev + tuple((group, plane(dy, dx)) for dy, dx in OFFSETS):
        pl.semaphore_signal(barrier, inc=1, device_id=peer, device_id_type=MESH)

    owners = [owner[group * BLOCKS + m] for m in range(BLOCKS)]
    places = []
    for m in range(BLOCKS):
        place = jnp.int32(0)
        for earlier in range(m):
            place = place + jnp.where(owners[earlier] == owners[m], 1, 0).astype(jnp.int32)
        places.append(jnp.minimum(place, SLOTS - 1))
    keys = [owners[m] * SLOTS + places[m] for m in range(BLOCKS)]

    def table(slot, carry):
        index, valid = jnp.int32(0), jnp.float32(0)
        for m in range(BLOCKS):
            hit = keys[m] == slot
            index = jnp.where(hit, m, index)
            valid = jnp.where(hit, 1.0, valid)
        idx_tab[slot] = index
        val_tab[slot] = valid
        return carry

    lax.fori_loop(0, NF * SLOTS, table, 0)

    pl.semaphore_wait(barrier, 3 + len(OFFSETS))

    sib_copy = [
        pltpu.make_async_remote_copy(
            src_ref=grads.at[z_of(j), 1 - c], dst_ref=sib.at[z_of(j)], send_sem=sib_ssem.at[j],
            recv_sem=sib_rsem.at[j], device_id=sibling, device_id_type=MESH)
        for j in range(NZ)
    ]
    for j in SIB_ORDER:
        sib_copy[j].start()

    def send_momentum(chunk):
        row = chunk * CHUNK
        for dy, dx in OFFSETS:
            to = plane(dy, dx)
            pltpu.make_async_remote_copy(
                src_ref=mom.at[:, pl.ds(pl.multiple_of(to * PIECE + row, CHUNK), CHUNK)],
                dst_ref=mrecv.at[f, :, pl.ds(pl.multiple_of(row, CHUNK), CHUNK)],
                send_sem=m_ssem, recv_sem=m_rsem, device_id=(group, to), device_id_type=MESH).start()

    def pair_sum(at, first, count):
        rows = pl.ds(pl.multiple_of(first, 16), count)
        return own[at, :, rows, :].astype(F32) + sib[at, :, rows, :].astype(F32)

    def first_copy(d, p):
        return pltpu.make_async_remote_copy(
            src_ref=s0.at[d, p], dst_ref=rz.at[d, 0, p, :, pl.ds(HALF * d, HALF)], send_sem=z_ssem.at[d, 0, p],
            recv_sem=z_rsem.at[d, 0, p], device_id=z_dev[d], device_id_type=MESH)

    def z_copy(d, t, p):
        if t == 0:
            return first_copy(d, p)
        return pltpu.make_async_remote_copy(
            src_ref=rz.at[d, t - 1, p], dst_ref=rz.at[d, t, p], send_sem=z_ssem.at[d, t, p],
            recv_sem=z_rsem.at[d, t, p], device_id=z_dev[d], device_id_type=MESH)

    def arrive(j):
        own_copy[j].wait()
        sib_copy[j].wait_recv()

    send_momentum(jnp.int32(0))
    arrive(4)

    def start_chain(p, carry):
        for d in (RIGHT, LEFT):
            s0[d, p] = pair_sum(z_of(4), p * CHUNK + HALF * d, HALF)
            z_copy(d, 0, p).start()
        return carry

    lax.fori_loop(0, NCH, start_chain, 0)

    def hop(t, p):
        for d in (RIGHT, LEFT):
            step = 4 - t if d == RIGHT else NZ - 4 + t

            @pl.when(p == 0)
            def _():
                arrive(step)

            at = z_of(step)
            z_copy(d, t - 1, p).wait_recv()
            if t == 1:
                other = 1 - d
                rz[d, 0, p, :, HALF * d:HALF * d + HALF, :] += pair_sum(at, p * CHUNK + HALF * d, HALF)
                rz[d, 0, p, :, HALF * other:HALF * other + HALF, :] = pair_sum(at, p * CHUNK + HALF * other, HALF)
            else:
                rz[d, t - 1, p] += pair_sum(at, p * CHUNK, CHUNK)
            z_copy(d, t, p).start()

    def finish(p):
        z_copy(RIGHT, 3, p).wait_recv()
        z_copy(LEFT, 3, p).wait_recv()
        rows = pl.ds(pl.multiple_of(p * CHUNK, CHUNK), CHUNK)
        gbuf[:, rows, :] = (pair_sum(z, p * CHUNK, CHUNK) + rz[RIGHT, 3, p] + rz[LEFT, 3, p]) * (1.0 / 16.0)

    def send_gradient(p):
        rows = pl.ds(pl.multiple_of(p * CHUNK, CHUNK), CHUNK)

        def fill(to, carry):
            for s in range(SLOTS):
                sendg[to, s, rows, :] = gbuf[idx_tab[to * SLOTS + s], rows, :] * val_tab[to * SLOTS + s]
            return carry

        lax.fori_loop(0, NF, fill, 0)
        target = pl.ds(pl.multiple_of(f * PIECE + p * CHUNK, CHUNK), CHUNK)
        for dy, dx in OFFSETS:
            to = plane(dy, dx)
            pltpu.make_async_remote_copy(
                src_ref=sendg.at[to, :, rows], dst_ref=grad_out.at[:, target],
                send_sem=g_ssem, recv_sem=g_rsem, device_id=(group, to), device_id_type=MESH).start()

    def slot(s, carry):
        for t in (1, 2, 3):
            p = s - t

            @pl.when((p >= 0) & (p < NCH))
            def _():
                hop(t, p)

        @pl.when(s < NCH)
        def _():
            send_momentum(s)

        @pl.when(s == 4)
        def _():
            arrive(0)

        @pl.when(s >= 4)
        def _():
            finish(s - 4)
            send_gradient(s - 4)

        return carry

    lax.fori_loop(1, NCH + 3, slot, 0)

    pltpu.make_async_copy(mrecv.at[pl.ds(0, NF - 1)], mrecv.at[pl.ds(0, NF - 1)], m_rsem).wait()
    mom_local.wait()

    def velocity(first, count):
        for m in range(BLOCKS):
            vbuf[m, first:first + count, :] = (1.0 + RATE) * gbuf[m, first:first + count, :] + (RATE * RATE) * mrecv[
                owners[m], places[m], first:first + count, :]

    def handler(b):
        return 2 * b + c

    def gram_copy(b):
        return pltpu.make_async_remote_copy(
            src_ref=gsend.at[b], dst_ref=grecv.at[f], send_sem=p_ssem.at[b], recv_sem=p_rsem,
            device_id=(group, handler(b)), device_id_type=MESH)

    def rows_copy(b):
        return pltpu.make_async_remote_copy(
            src_ref=vbuf.at[b, pl.ds(EARLY, CHUNK)], dst_ref=rrecv.at[f], send_sem=r_ssem.at[b], recv_sem=r_rsem,
            device_id=(group, handler(b)), device_id_type=MESH)

    velocity(0, EARLY)
    for b in range(BLOCKS):
        part = vbuf[b, 0:EARLY, :]
        gsend[b] = dot_t(part, part)

        @pl.when(handler(b) != f)
        def _():
            gram_copy(b).start()

    finish(NCH - 1)
    velocity(EARLY, CHUNK)
    for b in range(BLOCKS):
        @pl.when(handler(b) != f)
        def _():
            rows_copy(b).start()

    send_gradient(NCH - 1)
    grad_local = pltpu.make_async_copy(sendg.at[f], grad_out.at[:, pl.ds(f * PIECE, PIECE)], g_lsem)
    grad_local.start()

    mine = f // 2
    handles = f % 2 == c

    def q_copy(to):
        return pltpu.make_async_remote_copy(
            src_ref=qbuf.at[mine], dst_ref=qbuf.at[mine], send_sem=q_ssem, recv_sem=q_rsem.at[mine],
            device_id=(group, to), device_id_type=MESH)

    @pl.when(handles)
    def _():
        grecv[f] = gsend[mine]
        rrecv[f] = vbuf[mine, EARLY:PIECE, :]
        pltpu.make_async_copy(grecv.at[pl.ds(0, NF - 1)], grecv.at[pl.ds(0, NF - 1)], p_rsem).wait()
        gram = grecv[0]
        for i in range(1, NF):
            gram = gram + grecv[i]
        pltpu.make_async_copy(rrecv.at[pl.ds(0, NF - 1)], rrecv.at[pl.ds(0, NF - 1)], r_rsem).wait()
        late = rrecv[...].reshape(NF * CHUNK, R)
        gram = gram + dot_t(late, late)
        qbuf[mine] = polynomial(gram)
        for dy, dx in OFFSETS:
            q_copy(plane(dy, dx)).start()

    for b in range(BLOCKS):
        @pl.when(handler(b) != f)
        def _():
            pltpu.make_async_copy(qbuf.at[b], qbuf.at[b], q_rsem.at[b]).wait()

        update[b] = dot(vbuf[b], qbuf[b])

    @pl.when(handles)
    def _():
        pltpu.make_async_copy(grecv.at[pl.ds(0, NF - 1)], grecv.at[pl.ds(0, NF - 1)], q_ssem).wait()

    for b in range(BLOCKS):
        @pl.when(handler(b) != f)
        def _():
            gram_copy(b).wait_send()
            rows_copy(b).wait_send()

    for j in range(NZ):
        sib_copy[j].wait_send()

    def drain(p, carry):
        for d in (RIGHT, LEFT):
            for t in range(4):
                z_copy(d, t, p).wait_send()
        return carry

    lax.fori_loop(0, NCH, drain, 0)
    whole = sendg.at[pl.ds(0, NF - 1)]
    pltpu.make_async_copy(whole, whole, m_ssem).wait()
    pltpu.make_async_copy(whole, whole, g_ssem).wait()
    grad_local.wait()
    pltpu.make_async_copy(whole, whole, g_rsem).wait()


def local(grads, owner, momentum):
    raw = grads[0].reshape(NZ, 2, BLOCKS, PIECE, R)
    previous = momentum[0, 0]
    dma = pltpu.SemaphoreType.DMA
    update, gathered = pl.pallas_call(
        kernel,
        out_shape=(
            jax.ShapeDtypeStruct((BLOCKS, PIECE, R), F32),
            jax.ShapeDtypeStruct((SLOTS, D, R), F32),
        ),
        in_specs=[
            pl.BlockSpec(memory_space=pl.ANY),
            pl.BlockSpec(memory_space=pltpu.SMEM),
            pl.BlockSpec(memory_space=pl.ANY),
        ],
        out_specs=(pl.BlockSpec(memory_space=pltpu.VMEM), pl.BlockSpec(memory_space=pl.ANY)),
        scratch_shapes=[
            pltpu.VMEM((NZ, BLOCKS, PIECE, R), jnp.bfloat16),
            pltpu.VMEM((NZ, BLOCKS, PIECE, R), jnp.bfloat16),
            pltpu.VMEM((2, NCH, BLOCKS, HALF, R), F32),
            pltpu.VMEM((2, 4, NCH, BLOCKS, CHUNK, R), F32),
            pltpu.VMEM((NF, SLOTS, PIECE, R), F32),
            pltpu.VMEM((BLOCKS, PIECE, R), F32),
            pltpu.VMEM((BLOCKS, PIECE, R), F32),
            pltpu.VMEM((NF, SLOTS, PIECE, R), F32),
            pltpu.VMEM((BLOCKS, R, R), F32),
            pltpu.VMEM((NF, R, R), F32),
            pltpu.VMEM((NF, CHUNK, R), F32),
            pltpu.VMEM((BLOCKS, R, R), F32),
            pltpu.SMEM((NF * SLOTS,), jnp.int32),
            pltpu.SMEM((NF * SLOTS,), F32),
            dma((NZ,)), dma((NZ,)), dma((NZ,)),
            dma((2, 4, NCH)), dma((2, 4, NCH)),
            dma, dma, dma, dma, dma, dma,
            dma((BLOCKS,)), dma, dma((BLOCKS,)), dma, dma, dma((BLOCKS,)),
        ],
        compiler_params=pltpu.CompilerParams(
            collective_id=0, has_side_effects=True, vmem_limit_bytes=48 * 2**20),
    )(raw, owner[:, 0], previous)
    renewed = RATE * previous + gathered
    return update, renewed[None, None]


def solution(mesh):
    return jax.shard_map(
        local,
        mesh=mesh,
        in_specs=(P("dp", None, "fsdp", None), P(), P("dp", "fsdp", None, None, None)),
        out_specs=(P("dp", "fsdp", None), P("dp", "fsdp", None, None, None)),
        check_vma=False,
    )
```

time: 220 us -> 103 us (0.47)
  the two profiles are of different devices: /device:TPU:97 before, /device:TPU:2 now
where the time goes in v1:
time: 103 us; the launch traced here: 102 us
  Pallas kernels  96.5 us (94%)
  local copies, waits for them, and re-layouts  3.22 us (3%)
  other arithmetic  1.78 us (2%)
    pallas_call x1, Pallas kernels, local(): pl.pallas_call(kernel, out_shape=(jax.ShapeDtypeStruct((BLOCKS, PIECE, R)...  96.5 us
    unnamed x5, local copies, waits for them, and re-layouts  3.22 us

profile of v1, /device:TPU:2, one launch (start us, length us, event | category | flops | bytes accessed | tf_op | source)
XLA Modules:
  0.0 102.2 jit_solution(545837366163113708)
XLA Ops:
  0.6 0.0 copy-start
  0.6 1.7 %copy-done = f32[1,1,2,2560,128]{4,3,2,1,0:T(8,128)S(1)} copy-done((f32[1,1,2,2560,128]{4,3,2,1,0:T(8,128)S(1)}, f32[1,1,2,2560,128]{4,3,2,1,0:T(8,128)}, u32[]{:S(2)}) %copy-start) | copy-done | bytes 2621464
  2.4 0.0 copy-start.1
  2.4 0.7 copy-done.1
  3.0 96.5 %shard_map.50 = (f32[8,160,128]{2,1,0:T(8,128)S(1)}, f32[2,2560,128]{2,1,0:T(8,128)S(1)}) custom-call(bf16[8,2,8,160,128]{4,3,2,1,0:T(8,128)(2,1)} %bitcast.8, s32[128]{0:T(128)S(1)} %bitcast.7, f32[2,2560,128]{2,1,0:T(8,128)S(1)} %bitcast.6), custom_call_target="tpu_custom_call" | custom-call | tf_op jit(solution)/shard_map/pallas_call | solution.py:331
  99.6 1.8 %add_bitcast_fusion = f32[1,1,2,2560,128]{4,3,2,1,0:T(8,128)} fusion(f32[2,2560,128]{2,1,0:T(8,128)S(1)} %get-tuple-element.5, f32[1,1,2,2560,128]{4,3,2,1,0:T(8,128)S(1)} %copy-done), kind=kLoop, calls=%fused_computation | loop fusion | flops 1310720 | bytes 7864320 | tf_op jit(solution)/shard_map/broadcast_in_dim | solution.py:367
  101.3 0.8 copy.6
Async XLA Ops:
  0.6 1.7 %copy-start = (f32[1,1,2,2560,128]{4,3,2,1,0:T(8,128)S(1)}, f32[1,1,2,2560,128]{4,3,2,1,0:T(8,128)}, u32[]{:S(2)}) copy-start(f32[1,1,2,2560,128]{4,3,2,1,0:T(8,128)} %param.5) | copy-start | bytes 7864324
  2.4 0.7 copy-start.1

commit v2 on v0

v2 whole, which is shorter than its diff:
```python
import functools
import math

import jax
import jax.numpy as jnp
from jax import lax
from jax.experimental import pallas as pl
from jax.experimental.pallas import tpu as pltpu
from jax.sharding import PartitionSpec as P

MESH = pl.DeviceIdType.MESH
F32 = jnp.float32

NZ = 8
NA = 4
NF = NA * NA
BLOCKS = 8
SLOTS = 2
D = 2560
R = 128
PIECE = D // NF
CHUNK = 16
HALF = CHUNK // 2
NCH = PIECE // CHUNK
MID = PIECE // 2
EARLY_CH = 6
EARLY = EARLY_CH * CHUNK
LATE_CH = NCH - EARLY_CH
LEAD = 4
MERGE = 3
NEAR = 5
SPLIT = 16
PACKED = 72
ITERS = 3

COEF_A = 3.4445
COEF_B = -4.775
COEF_C = 2.0315
RATE = 0.95

OFFSETS = ((2, 2), (0, 2), (2, 0), (1, 2), (2, 1), (3, 2), (2, 3), (1, 1), (3, 3), (1, 3), (3, 1), (0, 1), (1, 0), (0, 3), (3, 0))
ORDER = (4, 3, 5, 2, 6, 1, 7, 0)
RIGHT, LEFT = 0, 1


def dot(a, b):
    return lax.dot_general(a, b, (((1,), (0,)), ((), ())), precision=lax.Precision.HIGHEST, preferred_element_type=F32)


def dot_t(a, b):
    return lax.dot_general(a, b, (((0,), (0,)), ((), ())), precision=lax.Precision.HIGHEST, preferred_element_type=F32)


def polynomial(gram):
    rows = lax.broadcasted_iota(jnp.int32, (R, R), 0)
    cols = lax.broadcasted_iota(jnp.int32, (R, R), 1)
    eye = jnp.where(rows == cols, 1.0, 0.0).astype(F32)
    total = jnp.sum(jnp.sum(gram * eye, axis=1, keepdims=True), axis=0, keepdims=True)
    inv = 1.0 / (jnp.sqrt(total) + 1e-07)
    gram = (gram * inv) * inv
    product = None
    for sweep in range(ITERS):
        poly = COEF_A * eye + COEF_B * gram + COEF_C * dot(gram, gram)
        product = poly if product is None else dot(product, poly)
        if sweep < ITERS - 1:
            gram = dot(poly, dot(gram, poly))
    return (0.2 * math.sqrt(D)) * inv * product


def pack(matrix):
    rows = lax.broadcasted_iota(jnp.int32, (R // 2, R), 0)
    cols = lax.broadcasted_iota(jnp.int32, (R // 2, R), 1)
    top, bottom = matrix[:R // 2], matrix[R // 2:]
    body = jnp.where(rows > cols, pltpu.roll(bottom, R // 2, 1), top)
    diagonal = jnp.sum(jnp.where(rows == cols - R // 2, bottom, 0.0), axis=0, keepdims=True)
    return body, jnp.broadcast_to(diagonal, (PACKED - R // 2, R))


def unpack(body, diagonal):
    rows = lax.broadcasted_iota(jnp.int32, (R // 2, R), 0)
    cols = lax.broadcasted_iota(jnp.int32, (R // 2, R), 1)
    turned = jnp.concatenate([body, jnp.zeros_like(body)], axis=0).T
    left = turned[:R // 2]
    top = jnp.where(rows <= cols, body, left)
    last = jnp.where(rows > cols - R // 2, pltpu.roll(body, R // 2, 1), pltpu.roll(left, R // 2, 1))
    last = jnp.where(rows == cols - R // 2, diagonal, last)
    bottom = jnp.where(cols < R // 2, turned[R // 2:], last)
    return jnp.concatenate([top, bottom], axis=0)


def remote(src, dst, send, recv, to):
    return pltpu.make_async_remote_copy(
        src_ref=src, dst_ref=dst, send_sem=send, recv_sem=recv, device_id=to, device_id_type=MESH)


def kernel(
    grads, owner, mom, update, renewed,
    who, raw, sib, r0, rz, momv, m1, m2s, m2r, m3s, m3r, gbuf, vbuf, gx, gr, gsend, grecv, rrecv, qbuf, idx_tab, val_tab,
    who_sem, raw_sem, mom_sem, sib_s, sib_r, t0_s, t0_r, z_s, z_r, m1_s, m1_r, m1_l, m2_ss, m2_rs, m3_ss, m3_rs,
    gx_s, gx_r, p_s, p_r, l_s, l_r, q_s, q_r,
):
    group = lax.axis_index("dp")
    f = lax.axis_index("fsdp")
    z, c = group // 2, group % 2
    me = (f // NA, f % NA)

    def z_of(step):
        return (z + step) % NZ

    def z_dev(d, core):
        return (z_of(1 if d == RIGHT else NZ - 1) * 2 + core, f)

    def plane(dy, dx):
        return ((me[0] + dy) % NA) * NA + (me[1] + dx) % NA

    def along(axis, step):
        return (group, plane(step, 0) if axis == 0 else plane(0, step))

    def on(axis, step):
        return (me[axis] + step) % NA

    def chunk(k):
        return pl.ds(pl.multiple_of(k * CHUNK, CHUNK), CHUNK)

    sibling = (z * 2 + 1 - c, f)

    who_copy = pltpu.make_async_copy(owner, who, who_sem)
    who_copy.start()
    raw_copy = [pltpu.make_async_copy(grads.at[z_of(j)], raw.at[z_of(j)], raw_sem.at[j]) for j in range(NZ)]
    for j in ORDER:
        raw_copy[j].start()
    mom_copy = pltpu.make_async_copy(mom, momv, mom_sem)
    mom_copy.start()

    barrier = pltpu.get_barrier_semaphore()
    peers = (sibling,) + tuple(z_dev(d, core) for d in (RIGHT, LEFT) for core in (c, 1 - c))
    peers += tuple((group, plane(dy, dx)) for dy, dx in OFFSETS)
    for peer in peers:
        pl.semaphore_signal(barrier, inc=1, device_id=peer, device_id_type=MESH)

    who_copy.wait()
    owners = [who[group * BLOCKS + m] for m in range(BLOCKS)]
    owner_at = ([lax.shift_right_logical(o, 2) for o in owners], [jnp.bitwise_and(o, 3) for o in owners])
    places = []
    for m in range(BLOCKS):
        place = jnp.int32(0)
        for earlier in range(m):
            place = place + jnp.where(owners[earlier] == owners[m], 1, 0).astype(jnp.int32)
        places.append(jnp.minimum(place, SLOTS - 1))
    keys = [owners[m] * SLOTS + places[m] for m in range(BLOCKS)]

    def table(slot, carry):
        index, valid = jnp.int32(0), jnp.float32(0)
        for m in range(BLOCKS):
            hit = keys[m] == slot
            index = jnp.where(hit, m, index)
            valid = jnp.where(hit, 1.0, valid)
        idx_tab[slot] = index
        val_tab[slot] = valid
        return carry

    lax.fori_loop(0, NF * SLOTS, table, 0)

    pl.semaphore_wait(barrier, len(peers))

    def t0_copies(k, q):
        return [
            remote(raw.at[z_of(4), core, :, chunk(k)], r0.at[k, i], t0_s.at[k, i], t0_r.at[k, i], z_dev(q, core))
            for i, core in enumerate((c, 1 - c))
        ]

    def z_copy(d, t, k):
        return remote(rz.at[d, t - 1, k], rz.at[d, t, k], z_s.at[d, t - 1, k], z_r.at[d, t - 1, k], z_dev(d, c))

    sib_copy = [
        None if j == 4 else remote(raw.at[z_of(j), 1 - c], sib.at[z_of(j)], sib_s.at[j], sib_r.at[j], sibling)
        for j in range(NZ)
    ]

    raw_copy[4].wait()
    for k in range(LEAD):
        for copy in t0_copies(k, k % 2):
            copy.start()
    for j in ORDER[1:]:
        raw_copy[j].wait()
        sib_copy[j].start()

    def m1_copy(h, j, first=0, count=MID):
        to = on(h, j)
        if h == 0:
            src = momv.at[:, to, :, pl.ds(first, count)]
        else:
            src = momv.at[:, :, to, pl.ds(MID + first, count)]
        dst = m1.at[h, me[h], :, :, pl.ds(first, count)]
        return remote(src, dst, m1_s.at[h, j - 1], m1_r.at[h, j - 1], along(h, j))

    def m1_local(h):
        if h == 0:
            src = momv.at[:, me[0], :, pl.ds(0, MID)]
        else:
            src = momv.at[:, :, me[1], pl.ds(MID, MID)]
        return pltpu.make_async_copy(src, m1.at[h, me[h]], m1_l.at[h])

    mom_copy.wait()
    for first in range(0, MID, SPLIT):
        for j in (2, 1, 3):
            for h in range(2):
                m1_copy(h, j, first, SPLIT).start()
    for h in range(2):
        m1_local(h).start()

    def held(h, step, m, first, count):
        b = 1 - h
        keep = jnp.where(owner_at[b][m] == me[b], 1.0, 0.0).astype(F32)
        return m1[h, owner_at[h][m], places[m], on(b, step), first:first + count, :] * keep

    def m2_copy(h, d):
        return remote(m2s.at[h, d], m2r.at[h, d], m2_ss.at[h, d], m2_rs.at[h, d], along(1 - h, 1 if d == RIGHT else 3))

    def m3_copy(h, d):
        return remote(m3s.at[h, d], m3r.at[h, d], m3_ss.at[h, d], m3_rs.at[h, d], along(1 - h, 1 if d == RIGHT else 3))

    QUARTER = MID // 2

    def merge_far():
        for h in range(2):
            for j in (1, 2, 3):
                m1_copy(h, j).wait_recv()
            m1_local(h).wait()
        for h in range(2):
            for d in (RIGHT, LEFT):
                for m in range(BLOCKS):
                    m2s[h, d, m] = held(h, 2, m, QUARTER * d, QUARTER)
                m2_copy(h, d).start()

    def merge_near():
        for h in range(2):
            for d in (RIGHT, LEFT):
                step = 1 if d == RIGHT else 3
                for m in range(BLOCKS):
                    m3s[h, d, m] = held(h, step, m, 0, MID)
                m2_copy(h, d).wait_recv()
                m3s[h, d, :, QUARTER * d:QUARTER * d + QUARTER, :] += m2r[h, d]
                m3_copy(h, d).start()

    def pair_sum(at, k):
        return raw[at, c, :, chunk(k), :].astype(F32) + sib[at, :, chunk(k), :].astype(F32)

    def hop(t, k, q):
        for d in (RIGHT, LEFT):
            step = 4 - t if d == RIGHT else NZ - 4 + t

            @pl.when(k == 0)
            def _():
                sib_copy[step].wait_recv()

            at = z_of(step)
            if t > 1:
                z_copy(d, t - 1, k).wait_recv()
                rz[d, t - 1, k] += pair_sum(at, k)
            elif d == q:
                for copy in t0_copies(k, q):
                    copy.wait_recv()
                rz[d, 0, k] = pair_sum(at, k) + (r0[k, 0].astype(F32) + r0[k, 1].astype(F32))
            else:
                rz[d, 0, k] = pair_sum(at, k)
            z_copy(d, t, k).start()

    def finish(k):
        z_copy(RIGHT, 3, k).wait_recv()
        z_copy(LEFT, 3, k).wait_recv()
        gbuf[:, chunk(k), :] = (pair_sum(z, k) + rz[RIGHT, 3, k] + rz[LEFT, 3, k]) * (1.0 / 16.0)

    def direct(pair):
        rows = pl.ds(pl.multiple_of(pair * 2 * CHUNK, 2 * CHUNK), 2 * CHUNK)

        def fill(to, carry):
            for s in range(SLOTS):
                gx[pair, to, s] = gbuf[idx_tab[to * SLOTS + s], rows, :] * val_tab[to * SLOTS + s]
            return carry

        lax.fori_loop(0, NF, fill, 0)
        for dy, dx in OFFSETS:
            to = plane(dy, dx)
            remote(gx.at[pair, to], gr.at[:, me[0], me[1], rows], gx_s, gx_r, (group, to)).start()
        gr[:, me[0], me[1], rows, :] = gx[pair, f]

    def velocity(first, count):
        for h in range(2):
            low, high = max(first, h * MID), min(first + count, (h + 1) * MID)
            if low >= high:
                continue
            at, n = low - h * MID, high - low
            for m in range(BLOCKS):
                state = held(h, 0, m, at, n) + m3r[h, RIGHT, m, at:at + n, :] + m3r[h, LEFT, m, at:at + n, :]
                vbuf[m, low:high, :] = (1.0 + RATE) * gbuf[m, low:high, :] + (RATE * RATE) * state

    def handler(b):
        return 2 * b + c

    def gram_copy(b):
        return remote(gsend.at[b], grecv.at[f], p_s.at[b], p_r, (group, handler(b)))

    def late_copy(i, b):
        rows = pl.ds(EARLY + i * CHUNK, CHUNK)
        return remote(vbuf.at[b, rows], rrecv.at[i, f], l_s.at[i, b], l_r.at[i], (group, handler(b)))

    def send_gram():
        for h in range(2):
            for d in (RIGHT, LEFT):
                m3_copy(h, d).wait_recv()
        velocity(0, EARLY)
        for b in range(BLOCKS):
            part = vbuf[b, 0:EARLY, :]
            body, diagonal = pack(dot_t(part, part))
            gsend[b, 0:R // 2, :] = body
            gsend[b, R // 2:PACKED, :] = diagonal

            @pl.when(handler(b) != f)
            def _():
                gram_copy(b).start()

    def send_late(i):
        velocity(EARLY + i * CHUNK, CHUNK)
        for b in range(BLOCKS):
            @pl.when(handler(b) != f)
            def _():
                late_copy(i, b).start()

    def when(k, run, low=0, high=NCH):
        @pl.when((k >= low) & (k < high))
        def _():
            run(k)

    def slots(sp, carry):
        for q in range(2):
            s = sp * 2 + q
            other = 1 - q
            when(s, lambda k: hop(1, k, q))
            when(s - 1, lambda k: hop(2, k, other))
            when(s - 2, lambda k: hop(3, k, q))

            @pl.when(s + LEAD < NCH)
            def _():
                for copy in t0_copies(s + LEAD, q):
                    copy.start()

            @pl.when(s == 3)
            def _():
                sib_copy[0].wait_recv()

            when(s - 3, finish)
            if q == 0:
                when(s - 4, lambda k: direct(k // 2), 0, NCH - 2)
            for at, run in (
                (MERGE, merge_far), (NEAR, merge_near), (2 + EARLY_CH, send_gram),
            ) + tuple((3 + EARLY_CH + i, functools.partial(send_late, i)) for i in range(LATE_CH - 1)):
                if at % 2 == q:
                    @pl.when(s == at)
                    def _():
                        run()
        return carry

    lax.fori_loop(0, (NCH + 2) // 2, slots, 0)

    last = NCH - 1
    finish(last)
    send_late(LATE_CH - 1)
    direct(NCH // 2 - 1)

    mine = f // 2
    handles = f % 2 == c

    def q_copy(to):
        return remote(qbuf.at[mine], qbuf.at[mine], q_s, q_r.at[mine], (group, to))

    @pl.when(handles)
    def _():
        grecv[f] = gsend[mine]
        for i in range(LATE_CH):
            rrecv[i, f] = vbuf[mine, EARLY + i * CHUNK:EARLY + (i + 1) * CHUNK, :]
        pltpu.make_async_copy(grecv.at[pl.ds(0, NF - 1)], grecv.at[pl.ds(0, NF - 1)], p_r).wait()
        total = grecv[0]
        for i in range(1, NF):
            total = total + grecv[i]
        gram = unpack(total[0:R // 2], total[R // 2:R // 2 + 1])
        for i in range(LATE_CH):
            pltpu.make_async_copy(rrecv.at[i, pl.ds(0, NF - 1)], rrecv.at[i, pl.ds(0, NF - 1)], l_r.at[i]).wait()
            late = rrecv[i].reshape(NF * CHUNK, R)
            gram = gram + dot_t(late, late)
        body, diagonal = pack(polynomial(gram))
        qbuf[mine, 0:R // 2, :] = body
        qbuf[mine, R // 2:PACKED, :] = diagonal
        for dy, dx in OFFSETS:
            q_copy(plane(dy, dx)).start()

    def receive_update():
        for b in range(BLOCKS):
            @pl.when(handler(b) != f)
            def _():
                pltpu.make_async_copy(qbuf.at[b], qbuf.at[b], q_r.at[b]).wait()

            update[b] = dot(vbuf[b], unpack(qbuf[b, 0:R // 2, :], qbuf[b, R // 2:R // 2 + 1, :]))

    def receive_gradient():
        part = gx.at[:, pl.ds(0, NF - 1)]
        pltpu.make_async_copy(part, part, gx_r).wait()
        for s in range(SLOTS):
            for a in range(NA):
                renewed[s, a] = RATE * momv[s, a] + gr[s, a]

    for b in range(BLOCKS):
        @pl.when(handler(b) != f)
        def _():
            gram_copy(b).wait_send()
            for i in range(LATE_CH):
                late_copy(i, b).wait_send()

    for j in ORDER[1:]:
        sib_copy[j].wait_send()
    for h in range(2):
        for j in (1, 2, 3):
            m1_copy(h, j).wait_send()
        for d in (RIGHT, LEFT):
            m2_copy(h, d).wait_send()
            m3_copy(h, d).wait_send()

    def drain(k, carry):
        for copy in t0_copies(k, 0):
            copy.wait_send()
        for d in (RIGHT, LEFT):
            for t in (1, 2, 3):
                z_copy(d, t, k).wait_send()
        return carry

    lax.fori_loop(0, NCH, drain, 0)
    receive_update()
    receive_gradient()

    @pl.when(handles)
    def _():
        part = grecv.at[pl.ds(0, NF - 1)]
        pltpu.make_async_copy(part, part, q_s).wait()

    part = gx.at[:, pl.ds(0, NF - 1)]
    pltpu.make_async_copy(part, part, gx_s).wait()


def place(update, renewed, update_out, renewed_out, sem):
    copies = (
        pltpu.make_async_copy(renewed, renewed_out, sem.at[0]),
        pltpu.make_async_copy(update, update_out, sem.at[1]),
    )
    for copy in copies:
        copy.start()
    for copy in copies:
        copy.wait()


def local(grads, owner, momentum):
    raw = grads[0].reshape(NZ, 2, BLOCKS, PIECE, R)
    previous = momentum[0, 0].reshape(SLOTS, NA, NA, PIECE, R)
    dma = pltpu.SemaphoreType.DMA

    def hbm(array):
        return pltpu.with_memory_space_constraint(array, pltpu.HBM)

    update, renewed = pl.pallas_call(
        kernel,
        out_shape=(
            pltpu.VMEM((BLOCKS, PIECE, R), F32),
            pltpu.VMEM((SLOTS, NA, NA, PIECE, R), F32),
        ),
        in_specs=[
            pl.BlockSpec(memory_space=pl.ANY),
            pl.BlockSpec(memory_space=pl.ANY),
            pl.BlockSpec(memory_space=pl.ANY),
        ],
        out_specs=(pl.BlockSpec(memory_space=pltpu.VMEM), pl.BlockSpec(memory_space=pltpu.VMEM)),
        scratch_shapes=[
            pltpu.SMEM((NF * BLOCKS,), jnp.int32),
            pltpu.VMEM((NZ, 2, BLOCKS, PIECE, R), jnp.bfloat16),
            pltpu.VMEM((NZ, BLOCKS, PIECE, R), jnp.bfloat16),
            pltpu.VMEM((NCH, 2, BLOCKS, CHUNK, R), jnp.bfloat16),
            pltpu.VMEM((2, 4, NCH, BLOCKS, CHUNK, R), F32),
            pltpu.VMEM((SLOTS, NA, NA, PIECE, R), F32),
            pltpu.VMEM((2, NA, SLOTS, NA, MID, R), F32),
            pltpu.VMEM((2, 2, BLOCKS, MID // 2, R), F32),
            pltpu.VMEM((2, 2, BLOCKS, MID // 2, R), F32),
            pltpu.VMEM((2, 2, BLOCKS, MID, R), F32),
            pltpu.VMEM((2, 2, BLOCKS, MID, R), F32),
            pltpu.VMEM((BLOCKS, PIECE, R), F32),
            pltpu.VMEM((BLOCKS, PIECE, R), F32),
            pltpu.VMEM((NCH // 2, NF, SLOTS, 2 * CHUNK, R), F32),
            pltpu.VMEM((SLOTS, NA, NA, PIECE, R), F32),
            pltpu.VMEM((BLOCKS, PACKED, R), F32),
            pltpu.VMEM((NF, PACKED, R), F32),
            pltpu.VMEM((LATE_CH, NF, CHUNK, R), F32),
            pltpu.VMEM((BLOCKS, PACKED, R), F32),
            pltpu.SMEM((NF * SLOTS,), jnp.int32),
            pltpu.SMEM((NF * SLOTS,), F32),
            dma, dma((NZ,)), dma, dma((NZ,)), dma((NZ,)),
            dma((NCH, 2)), dma((NCH, 2)), dma((2, 3, NCH)), dma((2, 3, NCH)),
            dma((2, 3)), dma((2, 3)), dma((2,)), dma((2, 2)), dma((2, 2)), dma((2, 2)), dma((2, 2)),
            dma, dma,
            dma((BLOCKS,)), dma, dma((LATE_CH, BLOCKS)), dma((LATE_CH,)), dma, dma((BLOCKS,)),
        ],
        compiler_params=pltpu.CompilerParams(
            collective_id=0, has_side_effects=True, vmem_limit_bytes=48 * 2**20),
    )(hbm(raw), hbm(owner[:, 0]), hbm(previous))
    update, renewed = pl.pallas_call(
        place,
        out_shape=(
            jax.ShapeDtypeStruct((BLOCKS, PIECE, R), F32),
            jax.ShapeDtypeStruct((SLOTS, NA, NA, PIECE, R), F32),
        ),
        in_specs=[pl.BlockSpec(memory_space=pl.ANY)] * 2,
        out_specs=(pl.BlockSpec(memory_space=pl.ANY),) * 2,
        scratch_shapes=[dma((2,))],
    )(pltpu.with_memory_space_constraint(update, pltpu.VMEM), pltpu.with_memory_space_constraint(renewed, pltpu.VMEM))
    return update, renewed.reshape(1, 1, SLOTS, D, R)


def solution(mesh):
    return jax.shard_map(
        local,
        mesh=mesh,
        in_specs=(P("dp", None, "fsdp", None), P(), P("dp", "fsdp", None, None, None)),
        out_specs=(P("dp", "fsdp", None), P("dp", "fsdp", None, None, None)),
        check_vma=False,
    )
```

time: 220 us -> 90.3 us (0.41)
  the two profiles are of different devices: /device:TPU:97 before, /device:TPU:2 now
where the time goes in v2:
time: 90.3 us; the launch traced here: 90.2 us
  Pallas kernels  89.5 us (99%)
    pallas_call x1, Pallas kernels, local(): pl.pallas_call(kernel, out_shape=(pltpu.VMEM((BLOCKS, PIECE, R), F32), pl...  87.8 us

profile of v2, /device:TPU:2, one launch (start us, length us, event | category | flops | bytes accessed | tf_op | source)
XLA Modules:
  0.0 90.2 jit_solution(4419291830594376014)
XLA Ops:
  0.6 87.8 %shard_map.50 = (f32[8,160,128]{2,1,0:T(8,128)S(1)}, f32[2,4,4,160,128]{4,3,2,1,0:T(8,128)S(1)}) custom-call(bf16[8,2,8,160,128]{4,3,2,1,0:T(8,128)(2,1)} %bitcast.4, s32[128]{0:T(128)} %bitcast.6, f32[2,4,4,160,128]{4,3,2,1,0:T(8,128)} %bitcast.5), custom_call_target="tpu_custom_call" | custom-call | tf_op jit(solution)/shard_map/pallas_call | solution.py:468
  88.5 1.7 %shard_map.51 = (f32[8,160,128]{2,1,0:T(8,128)}, f32[2,4,4,160,128]{4,3,2,1,0:T(8,128)}) custom-call(f32[8,160,128]{2,1,0:T(8,128)S(1)} %get-tuple-element.6.update, f32[2,4,4,160,128]{4,3,2,1,0:T(8,128)S(1)} %get-tuple-element.7.renewed), custom_call_target="tpu_custom_call" | custom-call | tf_op jit(solution)/shard_map/pallas_call | solution.py:511

commit v3 on v2

--- a/solution.py
+++ b/solution.py
@@ -29,7 +29,7 @@
 LEAD = 4
 MERGE = 3
 NEAR = 5
-SPLIT = 16
+SPLIT = 80
 PACKED = 72
 ITERS = 3
 
@@ -138,6 +138,54 @@
     for peer in peers:
         pl.semaphore_signal(barrier, inc=1, device_id=peer, device_id_type=MESH)
 
+    pl.semaphore_wait(barrier, len(peers))
+
+    def t0_copies(k, q):
+        return [
+            remote(raw.at[z_of(4), core, :, chunk(k)], r0.at[k, i], t0_s.at[k, i], t0_r.at[k, i], z_dev(q, core))
+            for i, core in enumerate((c, 1 - c))
+        ]
+
+    def z_copy(d, t, k):
+        return remote(rz.at[d, t - 1, k], rz.at[d, t, k], z_s.at[d, t - 1, k], z_r.at[d, t - 1, k], z_dev(d, c))
+
+    sib_copy = [
+        None if j == 4 else remote(raw.at[z_of(j), 1 - c], sib.at[z_of(j)], sib_s.at[j], sib_r.at[j], sibling)
+        for j in range(NZ)
+    ]
+
+    raw_copy[4].wait()
+    for k in range(LEAD):
+        for copy in t0_copies(k, k % 2):
+            copy.start()
+    for j in ORDER[1:]:
+        raw_copy[j].wait()
+        sib_copy[j].start()
+
+    def m1_copy(h, j, first=0, count=MID):
+        to = on(h, j)
+        if h == 0:
+            src = momv.at[:, to, :, pl.ds(first, count)]
+        else:
+            src = momv.at[:, :, to, pl.ds(MID + first, count)]
+        dst = m1.at[h, me[h], :, :, pl.ds(first, count)]
+        return remote(src, dst, m1_s.at[h, j - 1], m1_r.at[h, j - 1], along(h, j))
+
+    def m1_local(h):
+        if h == 0:
+            src = momv.at[:, me[0], :, pl.ds(0, MID)]
+        else:
+            src = momv.at[:, :, me[1], pl.ds(MID, MID)]
+        return pltpu.make_async_copy(src, m1.at[h, me[h]], m1_l.at[h])
+
+    mom_copy.wait()
+    for first in range(0, MID, SPLIT):
+        for j in (2, 1, 3):
+            for h in range(2):
+                m1_copy(h, j, first, SPLIT).start()
+    for h in range(2):
+        m1_local(h).start()
+
     who_copy.wait()
     owners = [who[group * BLOCKS + m] for m in range(BLOCKS)]
     owner_at = ([lax.shift_right_logical(o, 2) for o in owners], [jnp.bitwise_and(o, 3) for o in owners])
@@ -160,54 +208,6 @@
         return carry
 
     lax.fori_loop(0, NF * SLOTS, table, 0)
-
-    pl.semaphore_wait(barrier, len(peers))
-
-    def t0_copies(k, q):
-        return [
-            remote(raw.at[z_of(4), core, :, chunk(k)], r0.at[k, i], t0_s.at[k, i], t0_r.at[k, i], z_dev(q, core))
-            for i, core in enumerate((c, 1 - c))
-        ]
-
-    def z_copy(d, t, k):
-        return remote(rz.at[d, t - 1, k], rz.at[d, t, k], z_s.at[d, t - 1, k], z_r.at[d, t - 1, k], z_dev(d, c))
-
-    sib_copy = [
-        None if j == 4 else remote(raw.at[z_of(j), 1 - c], sib.at[z_of(j)], sib_s.at[j], sib_r.at[j], sibling)
-        for j in range(NZ)
-    ]
-
-    raw_copy[4].wait()
-    for k in range(LEAD):
-        for copy in t0_copies(k, k % 2):
-            copy.start()
-    for j in ORDER[1:]:
-        raw_copy[j].wait()
-        sib_copy[j].start()
-
-    def m1_copy(h, j, first=0, count=MID):
-        to = on(h, j)
-        if h == 0:
-            src = momv.at[:, to, :, pl.ds(first, count)]
-        else:
-            src = momv.at[:, :, to, pl.ds(MID + first, count)]
-        dst = m1.at[h, me[h], :, :, pl.ds(first, count)]
-        return remote(src, dst, m1_s.at[h, j - 1], m1_r.at[h, j - 1], along(h, j))
-
-    def m1_local(h):
-        if h == 0:
-            src = momv.at[:, me[0], :, pl.ds(0, MID)]
-        else:
-            src = momv.at[:, :, me[1], pl.ds(MID, MID)]
-        return pltpu.make_async_copy(src, m1.at[h, me[h]], m1_l.at[h])
-
-    mom_copy.wait()
-    for first in range(0, MID, SPLIT):
-        for j in (2, 1, 3):
-            for h in range(2):
-                m1_copy(h, j, first, SPLIT).start()
-    for h in range(2):
-        m1_local(h).start()
 
     def held(h, step, m, first, count):
         b = 1 - h
@@ -271,19 +271,19 @@
         z_copy(LEFT, 3, k).wait_recv()
         gbuf[:, chunk(k), :] = (pair_sum(z, k) + rz[RIGHT, 3, k] + rz[LEFT, 3, k]) * (1.0 / 16.0)
 
-    def direct(pair):
-        rows = pl.ds(pl.multiple_of(pair * 2 * CHUNK, 2 * CHUNK), 2 * CHUNK)
+    def direct(first, count):
+        rows = pl.ds(pl.multiple_of(first, CHUNK), count)
 
         def fill(to, carry):
             for s in range(SLOTS):
-                gx[pair, to, s] = gbuf[idx_tab[to * SLOTS + s], rows, :] * val_tab[to * SLOTS + s]
+                gx[to, s, rows, :] = gbuf[idx_tab[to * SLOTS + s], rows, :] * val_tab[to * SLOTS + s]
             return carry
 
         lax.fori_loop(0, NF, fill, 0)
         for dy, dx in OFFSETS:
             to = plane(dy, dx)
-            remote(gx.at[pair, to], gr.at[:, me[0], me[1], rows], gx_s, gx_r, (group, to)).start()
-        gr[:, me[0], me[1], rows, :] = gx[pair, f]
+            remote(gx.at[to, :, rows], gr.at[:, me[0], me[1], rows], gx_s, gx_r, (group, to)).start()
+        gr[:, me[0], me[1], rows, :] = gx[f, :, rows, :]
 
     def velocity(first, count):
         for h in range(2):
@@ -332,6 +332,8 @@
         def _():
             run(k)
 
+    last = NCH - 1
+
     def slots(sp, carry):
         for q in range(2):
             s = sp * 2 + q
@@ -351,7 +353,7 @@
 
             when(s - 3, finish)
             if q == 0:
-                when(s - 4, lambda k: direct(k // 2), 0, NCH - 2)
+                when(s - 4, lambda k: direct(k * CHUNK, 2 * CHUNK), 0, NCH - 2)
             for at, run in (
                 (MERGE, merge_far), (NEAR, merge_near), (2 + EARLY_CH, send_gram),
             ) + tuple((3 + EARLY_CH + i, functools.partial(send_late, i)) for i in range(LATE_CH - 1)):
@@ -363,10 +365,9 @@
 
     lax.fori_loop(0, (NCH + 2) // 2, slots, 0)
 
-    last = NCH - 1
     finish(last)
     send_late(LATE_CH - 1)
-    direct(NCH // 2 - 1)
+    direct((last - 1) * CHUNK, CHUNK)
 
     mine = f // 2
     handles = f % 2 == c
@@ -403,7 +404,7 @@
             update[b] = dot(vbuf[b], unpack(qbuf[b, 0:R // 2, :], qbuf[b, R // 2:R // 2 + 1, :]))
 
     def receive_gradient():
-        part = gx.at[:, pl.ds(0, NF - 1)]
+        part = gx.at[pl.ds(0, NF - 1)]
         pltpu.make_async_copy(part, part, gx_r).wait()
         for s in range(SLOTS):
             for a in range(NA):
@@ -434,6 +435,7 @@
         return carry
 
     lax.fori_loop(0, NCH, drain, 0)
+    direct(last * CHUNK, CHUNK)
     receive_update()
     receive_gradient()
 
@@ -442,15 +444,17 @@
         part = grecv.at[pl.ds(0, NF - 1)]
         pltpu.make_async_copy(part, part, q_s).wait()
 
-    part = gx.at[:, pl.ds(0, NF - 1)]
+    part = gx.at[pl.ds(0, NF - 1)]
     pltpu.make_async_copy(part, part, gx_s).wait()
 
 
 def place(update, renewed, update_out, renewed_out, sem):
-    copies = (
-        pltpu.make_async_copy(renewed, renewed_out, sem.at[0]),
-        pltpu.make_async_copy(update, update_out, sem.at[1]),
-    )
+    copies = []
+    for i in range(BLOCKS):
+        copies.append(pltpu.make_async_copy(renewed.at[i // 4, i % 4], renewed_out.at[i // 4, i % 4], sem.at[i]))
+    for i in range(2):
+        half = pl.ds(i * (BLOCKS // 2), BLOCKS // 2)
+        copies.append(pltpu.make_async_copy(update.at[half], update_out.at[half], sem.at[BLOCKS + i]))
     for copy in copies:
         copy.start()
     for copy in copies:
@@ -491,7 +495,7 @@
             pltpu.VMEM((2, 2, BLOCKS, MID, R), F32),
             pltpu.VMEM((BLOCKS, PIECE, R), F32),
             pltpu.VMEM((BLOCKS, PIECE, R), F32),
-            pltpu.VMEM((NCH // 2, NF, SLOTS, 2 * CHUNK, R), F32),
+            pltpu.VMEM((NF, SLOTS, PIECE, R), F32),
             pltpu.VMEM((SLOTS, NA, NA, PIECE, R), F32),
             pltpu.VMEM((BLOCKS, PACKED, R), F32),
             pltpu.VMEM((NF, PACKED, R), F32),
@@ -516,7 +520,7 @@
         ),
         in_specs=[pl.BlockSpec(memory_space=pl.ANY)] * 2,
         out_specs=(pl.BlockSpec(memory_space=pl.ANY),) * 2,
-        scratch_shapes=[dma((2,))],
+        scratch_shapes=[dma((BLOCKS + 2,))],
     )(pltpu.with_memory_space_constraint(update, pltpu.VMEM), pltpu.with_memory_space_constraint(renewed, pltpu.VMEM))
     return update, renewed.reshape(1, 1, SLOTS, D, R)
 

time: 90.3 us -> 89 us (0.986)
  Pallas kernels: 89.5 us -> 88.3 us
    pallas_call x1, Pallas kernels: 87.8 us -> 86.5 us  [local(): pl.pallas_call(kernel, out_shape=(pltpu.VMEM((BLOCKS, PIECE, R), F32), pl...]
where the time goes in v3:
time: 89 us; the launch traced here: 88.9 us
  Pallas kernels  88.3 us (99%)
    pallas_call x1, Pallas kernels, local(): pl.pallas_call(kernel, out_shape=(pltpu.VMEM((BLOCKS, PIECE, R), F32), pl...  86.5 us
    pallas_call x1, Pallas kernels, local(): pl.pallas_call(place, out_shape=(jax.ShapeDtypeStruct((BLOCKS, PIECE, R),...  1.78 us

profile of v3, /device:TPU:2, one launch (start us, length us, event | category | flops | bytes accessed | tf_op | source)
XLA Modules:
  0.0 88.9 jit_solution(16837809243087925294)
XLA Ops:
  0.6 86.5 %shard_map.50 = (f32[8,160,128]{2,1,0:T(8,128)S(1)}, f32[2,4,4,160,128]{4,3,2,1,0:T(8,128)S(1)}) custom-call(bf16[8,2,8,160,128]{4,3,2,1,0:T(8,128)(2,1)} %bitcast.4, s32[128]{0:T(128)} %bitcast.6, f32[2,4,4,160,128]{4,3,2,1,0:T(8,128)} %bitcast.5), custom_call_target="tpu_custom_call" | custom-call | tf_op jit(solution)/shard_map/pallas_call | solution.py:472
  87.1 1.8 %shard_map.51 = (f32[8,160,128]{2,1,0:T(8,128)}, f32[2,4,4,160,128]{4,3,2,1,0:T(8,128)}) custom-call(f32[8,160,128]{2,1,0:T(8,128)S(1)} %get-tuple-element.6.update, f32[2,4,4,160,128]{4,3,2,1,0:T(8,128)S(1)} %get-tuple-element.7.renewed), custom_call_target="tpu_custom_call" | custom-call | tf_op jit(solution)/shard_map/pallas_call | solution.py:515

commit v4 on v3

--- a/solution.py
+++ b/solution.py
@@ -352,8 +352,7 @@
                 sib_copy[0].wait_recv()
 
             when(s - 3, finish)
-            if q == 0:
-                when(s - 4, lambda k: direct(k * CHUNK, 2 * CHUNK), 0, NCH - 2)
+            when(s - 3, lambda k: direct(k * CHUNK, CHUNK), 0, NCH - 2)
             for at, run in (
                 (MERGE, merge_far), (NEAR, merge_near), (2 + EARLY_CH, send_gram),
             ) + tuple((3 + EARLY_CH + i, functools.partial(send_late, i)) for i in range(LATE_CH - 1)):

time: 89 us -> 87.5 us (0.983)
  Pallas kernels: 88.3 us -> 86.8 us
    pallas_call x1, Pallas kernels: 86.5 us -> 85 us  [local(): pl.pallas_call(kernel, out_shape=(pltpu.VMEM((BLOCKS, PIECE, R), F32), pl...]
where the time goes in v4:
time: 87.5 us
  Pallas kernels  86.8 us (99%)
    pallas_call x1, Pallas kernels, local(): pl.pallas_call(kernel, out_shape=(pltpu.VMEM((BLOCKS, PIECE, R), F32), pl...  85 us
    pallas_call x1, Pallas kernels, local(): pl.pallas_call(place, out_shape=(jax.ShapeDtypeStruct((BLOCKS, PIECE, R),...  1.78 us

profile of v4, /device:TPU:2, one launch (start us, length us, event | category | flops | bytes accessed | tf_op | source)
XLA Modules:
  0.0 87.5 jit_solution(9675680344891914491)
XLA Ops:
  0.6 85.0 %shard_map.50 = (f32[8,160,128]{2,1,0:T(8,128)S(1)}, f32[2,4,4,160,128]{4,3,2,1,0:T(8,128)S(1)}) custom-call(bf16[8,2,8,160,128]{4,3,2,1,0:T(8,128)(2,1)} %bitcast.4, s32[128]{0:T(128)} %bitcast.6, f32[2,4,4,160,128]{4,3,2,1,0:T(8,128)} %bitcast.5), custom_call_target="tpu_custom_call" | custom-call | tf_op jit(solution)/shard_map/pallas_call | solution.py:471
  85.7 1.8 %shard_map.51 = (f32[8,160,128]{2,1,0:T(8,128)}, f32[2,4,4,160,128]{4,3,2,1,0:T(8,128)}) custom-call(f32[8,160,128]{2,1,0:T(8,128)S(1)} %get-tuple-element.6.update, f32[2,4,4,160,128]{4,3,2,1,0:T(8,128)S(1)} %get-tuple-element.7.renewed), custom_call_target="tpu_custom_call" | custom-call | tf_op jit(solution)/shard_map/pallas_call | solution.py:514

commit v5 on v4

--- a/solution.py
+++ b/solution.py
@@ -95,7 +95,7 @@
 
 def kernel(
     grads, owner, mom, update, renewed,
-    who, raw, sib, r0, rz, momv, m1, m2s, m2r, m3s, m3r, gbuf, vbuf, gx, gr, gsend, grecv, rrecv, qbuf, idx_tab, val_tab,
+    who, raw, sib, r0, rz, momv, m1, m2s, m2r, m3s, m3r, gbuf, vbuf, gx, gr, gsend, grecv, rrecv, held_gram, qbuf, idx_tab, val_tab,
     who_sem, raw_sem, mom_sem, sib_s, sib_r, t0_s, t0_r, z_s, z_r, m1_s, m1_r, m1_l, m2_ss, m2_rs, m3_ss, m3_rs,
     gx_s, gx_r, p_s, p_r, l_s, l_r, q_s, q_r,
 ):
@@ -364,30 +364,39 @@
 
     lax.fori_loop(0, (NCH + 2) // 2, slots, 0)
 
-    finish(last)
-    send_late(LATE_CH - 1)
-    direct((last - 1) * CHUNK, CHUNK)
-
     mine = f // 2
     handles = f % 2 == c
 
-    def q_copy(to):
-        return remote(qbuf.at[mine], qbuf.at[mine], q_s, q_r.at[mine], (group, to))
+    def late_gram(i):
+        rrecv[i, f] = vbuf[mine, EARLY + i * CHUNK:EARLY + (i + 1) * CHUNK, :]
+        pltpu.make_async_copy(rrecv.at[i, pl.ds(0, NF - 1)], rrecv.at[i, pl.ds(0, NF - 1)], l_r.at[i]).wait()
+        late = rrecv[i].reshape(NF * CHUNK, R)
+        return dot_t(late, late)
 
     @pl.when(handles)
     def _():
         grecv[f] = gsend[mine]
-        for i in range(LATE_CH):
-            rrecv[i, f] = vbuf[mine, EARLY + i * CHUNK:EARLY + (i + 1) * CHUNK, :]
         pltpu.make_async_copy(grecv.at[pl.ds(0, NF - 1)], grecv.at[pl.ds(0, NF - 1)], p_r).wait()
         total = grecv[0]
         for i in range(1, NF):
             total = total + grecv[i]
         gram = unpack(total[0:R // 2], total[R // 2:R // 2 + 1])
-        for i in range(LATE_CH):
-            pltpu.make_async_copy(rrecv.at[i, pl.ds(0, NF - 1)], rrecv.at[i, pl.ds(0, NF - 1)], l_r.at[i]).wait()
-            late = rrecv[i].reshape(NF * CHUNK, R)
-            gram = gram + dot_t(late, late)
+        for i in range(LATE_CH - 2):
+            gram = gram + late_gram(i)
+        held_gram[...] = gram
+
+    finish(last)
+    send_late(LATE_CH - 1)
+    direct((last - 1) * CHUNK, CHUNK)
+
+    def q_copy(to):
+        return remote(qbuf.at[mine], qbuf.at[mine], q_s, q_r.at[mine], (group, to))
+
+    @pl.when(handles)
+    def _():
+        gram = held_gram[...]
+        for i in range(LATE_CH - 2, LATE_CH):
+            gram = gram + late_gram(i)
         body, diagonal = pack(polynomial(gram))
         qbuf[mine, 0:R // 2, :] = body
         qbuf[mine, R // 2:PACKED, :] = diagonal
@@ -499,6 +508,7 @@
             pltpu.VMEM((BLOCKS, PACKED, R), F32),
             pltpu.VMEM((NF, PACKED, R), F32),
             pltpu.VMEM((LATE_CH, NF, CHUNK, R), F32),
+            pltpu.VMEM((R, R), F32),
             pltpu.VMEM((BLOCKS, PACKED, R), F32),
             pltpu.SMEM((NF * SLOTS,), jnp.int32),
             pltpu.SMEM((NF * SLOTS,), F32),

time: 87.5 us -> 91.7 us (1.048)
  Pallas kernels: 86.8 us -> 91 us
    pallas_call x1, Pallas kernels: 85 us -> 89.2 us  [local(): pl.pallas_call(kernel, out_shape=(pltpu.VMEM((BLOCKS, PIECE, R), F32), pl...]
where the time goes in v5:
time: 91.7 us; the launch traced here: 91.6 us
  Pallas kernels  91 us (99%)
    pallas_call x1, Pallas kernels, local(): pl.pallas_call(kernel, out_shape=(pltpu.VMEM((BLOCKS, PIECE, R), F32), pl...  89.2 us

profile of v5, /device:TPU:2, one launch (start us, length us, event | category | flops | bytes accessed | tf_op | source)
XLA Modules:
  0.0 91.6 jit_solution(6851695864442447955)
XLA Ops:
  0.6 89.2 %shard_map.50 = (f32[8,160,128]{2,1,0:T(8,128)S(1)}, f32[2,4,4,160,128]{4,3,2,1,0:T(8,128)S(1)}) custom-call(bf16[8,2,8,160,128]{4,3,2,1,0:T(8,128)(2,1)} %bitcast.4, s32[128]{0:T(128)} %bitcast.6, f32[2,4,4,160,128]{4,3,2,1,0:T(8,128)} %bitcast.5), custom_call_target="tpu_custom_call" | custom-call | tf_op jit(solution)/shard_map/pallas_call | solution.py:480
  89.8 1.8 %shard_map.51 = (f32[8,160,128]{2,1,0:T(8,128)}, f32[2,4,4,160,128]{4,3,2,1,0:T(8,128)}) custom-call(f32[8,160,128]{2,1,0:T(8,128)S(1)} %get-tuple-element.6.update, f32[2,4,4,160,128]{4,3,2,1,0:T(8,128)S(1)} %get-tuple-element.7.renewed), custom_call_target="tpu_custom_call" | custom-call | tf_op jit(solution)/shard_map/pallas_call | solution.py:524
